TPU v7x, 32 devices: a whole 2x2x4 slice. The times are simulated.
32 devices in a mesh: groups: 2 (over x), blk: 16 (over z, y, core).
Axes of the slice: x: 2, y: 2, z: 4, core: 2. Of those that a mesh axis runs over, the one named last changes fastest.
Arguments:
- tokens: int32 [4, 64], P(None, 'groups'), parts along dimension 1, may hold values from 0 to 255
- alpha_start: bfloat16 [64, 262144], P('groups', 'blk'), parts along dimension 0, may hold values from 0.25 to 4, as said below
- beta_in: bfloat16 [64, 262144], P('groups', 'blk'), parts along dimension 0, may hold values from 0.25 to 4, as said below
- emission: bfloat16 [256, 512], replicated, may hold values from 0.0099487305 to 1
- left_factor: bfloat16 [512, 512, 512], P('blk'), may hold values from 1.953125e-10 to 0.05859375, as said below
- right_factor: bfloat16 [512, 512, 512], P('blk'), may hold values from 1.953125e-10 to 0.05859375, as said below
Outputs:
- count_left: bfloat16 [1024, 512, 512], P(('groups', 'blk')), parts along dimension 0
- beta_out: bfloat16 [64, 262144], P('groups', 'blk'), parts along dimension 0
- log_scales: float32 [3, 64], P(None, 'groups'), parts along dimension 1
There are 2 independent parts, one for each index of `groups`. A program takes and returns all parts, laid end to end along the dimension named above; an argument that names none is the same for every part. Nothing has to cross between parts.
Inputs may be any that keep to these rules, and one draw needn't show every extreme that they name: `left_factor`: every entry is positive. `right_factor`: every entry is positive. `alpha_start`: every entry is positive. `beta_in`: every entry is positive.
All inputs are finite; a program needn't handle non-finite values.
Results may differ from a plain program's by a relative error of at most 0.0045.
Values may be sent and summed in bfloat16 or wider, within the bound.
A program may use at most 192 MiB of HBM per device.

v0:
```python
import jax
import jax.numpy as jnp
from jax import lax
from jax.sharding import PartitionSpec as P


def on_device(tokens, alpha_start, beta_in, emission, left_factor, right_factor):
    blocks_dev, block_size, _ = left_factor.shape
    seq_count = alpha_start.shape[0]
    window = tokens.shape[0]
    vocab_size = emission.shape[0]
    states = block_size * block_size

    def emission_rows(step):
        picked = tokens[step][:, None] == lax.broadcasted_iota(
            jnp.int32, (seq_count, vocab_size), 1
        )
        rows = jnp.dot(picked.astype(jnp.bfloat16), emission, preferred_element_type=jnp.float32)
        return rows[None, :, :]

    def path_sums(message):
        return jnp.einsum(
            "rns,rsp->rnp", message, right_factor, preferred_element_type=jnp.float32
        ).astype(jnp.bfloat16)

    forward_msg = jnp.transpose(alpha_start.reshape(seq_count, blocks_dev, block_size), (1, 0, 2))
    forwards = [forward_msg]
    received = []
    log_rows = []
    for step in range(1, window):
        arrived = lax.all_to_all(
            path_sums(forward_msg), "blk", split_axis=2, concat_axis=0, tiled=True
        )
        turned_paths = jnp.transpose(arrived, (2, 1, 0))
        received.append(turned_paths)
        ahead = jnp.einsum(
            "pnr,prq->pnq", turned_paths, left_factor, preferred_element_type=jnp.float32
        )
        weighted = ahead * emission_rows(step - 1)
        forward_total = lax.psum(jnp.sum(weighted, axis=(0, 2)), "blk")
        log_rows.append(jnp.log(forward_total / states))
        forward_msg = (states * weighted / forward_total[None, :, None]).astype(jnp.bfloat16)
        forwards.append(forward_msg)
    last_send = path_sums(forward_msg)
    received.append(
        jnp.transpose(
            lax.all_to_all(last_send, "blk", split_axis=2, concat_axis=0, tiled=True), (2, 1, 0)
        )
    )
    backward_msg = jnp.transpose(beta_in.reshape(seq_count, blocks_dev, block_size), (1, 0, 2))
    weights = []
    values = []
    for step in range(window, 0, -1):
        emitted = (emission_rows(step - 1) * backward_msg).astype(jnp.bfloat16)
        back_sums = jnp.einsum(
            "pnq,prq->pnr", emitted, left_factor, preferred_element_type=jnp.float32
        ).astype(jnp.bfloat16)
        if step == window:
            turned = lax.all_to_all(back_sums, "blk", split_axis=2, concat_axis=0, tiled=True)
        else:
            turned = lax.all_to_all(back_sums, "blk", split_axis=2, concat_axis=0, tiled=True)
        turned_back = jnp.transpose(turned, (2, 1, 0))
        prior = jnp.einsum(
            "rnp,rsp->rns", turned_back, right_factor, preferred_element_type=jnp.float32
        )
        norm_total, posterior_total = lax.psum(
            (jnp.sum(prior, axis=(0, 2)), jnp.sum(forwards[step - 1] * prior, axis=(0, 2))), "blk"
        )
        weights.append(
            (received[step - 1].astype(jnp.float32) / posterior_total[None, :, None]).astype(
                jnp.bfloat16
            )
        )
        values.append(emitted)
        backward_msg = (states * prior / norm_total[None, :, None]).astype(jnp.bfloat16)
    stacked_weights = jnp.concatenate(weights, axis=1)
    stacked_values = jnp.concatenate(values, axis=1)
    tally = jnp.einsum(
        "pnr,pnq->prq", stacked_weights, stacked_values, preferred_element_type=jnp.float32
    )
    count_left = (left_factor * tally * (block_size * states / seq_count)).astype(jnp.bfloat16)
    log_scales = jnp.stack(log_rows, axis=0)
    beta_out = jnp.transpose(backward_msg, (1, 0, 2)).reshape(seq_count, blocks_dev * block_size)
    return (count_left, beta_out, log_scales)


def solution(mesh):
    in_specs = (
        P(None, "groups"),
        P("groups", "blk"),
        P("groups", "blk"),
        P(),
        P("blk", None, None),
        P("blk", None, None),
    )
    out_specs = (P(("groups", "blk"), None, None), P("groups", "blk"), P(None, "groups"))
    return jax.shard_map(
        on_device, mesh=mesh, in_specs=in_specs, out_specs=out_specs, check_vma=False
    )
```

profile of v0, /device:TPU:0, one launch (start us, length us, event | category | flops | bytes accessed | tf_op | source)
XLA Modules:
  0.0 797.4 jit_solution(8956417036194098594)
XLA Ops:
  0.6 8.7 %convolution_convert_fusion.7 = bf16[32,32,512]{2,1,0:T(8,128)(2,1)S(1)} fusion(bf16[32,512,512]{2,1,0:T(8,128)(2,1)} %param.11, bf16[4,32,8,512]{3,2,1,0:T(8,128)(2,1)} %bitcast.191), kind=kOutput, calls=%fused_computation.45 | convolution fusion | flops 537395200 | bytes 18874368 | tf_op jit(solution)/shard_map/rns,rsp->rnp/dot_general | solution.py:22
  9.4 6.5 copy.31
  15.8 7.4 reshape.43
  23.3 7.5 all-to-all-start
  31.0 22.7 %all-to-all-done = bf16[16,2,16384]{2,1,0:T(2,128)(2,1)S(1)} async-done(((bf16[16,2,16384]{2,1,0:T(2,128)(2,1)}), bf16[16,2,16384]{2,1,0:T(2,128)(2,1)S(1)}, u32[]{:S(2)}, u32[]{:S(2)}) %all-to-all-start) | async-done | bytes 1048608 | tf_op jit(solution)/shard_map/all_to_all | solution.py:31
  57.2 6.7 copy.32
  69.9 8.6 %multiply_reduce_fusion.6 = (f32[32]{0:T(128)S(1)}, f32[32,32,512]{2,1,0:T(8,128)S(1)}) fusion(f32[32,512]{1,0:T(8,128)S(1)} %fusion.33, bf16[32,512,512]{2,1,0:T(8,128)(2,1)} %param.10, bf16[512,32,32]{0,1,2:T(8,128)(2,1)S(1)} %all_to_all.101), kind=kOutput, calls=%fused_computation.37 | convolution fusion | flops 537919488 | bytes 19988608 | tf_op jit(solution)/shard_map/pnr,prq->pnq/dot_general | solution.py:36
  78.5 35.3 %psum.77 = f32[32]{0:T(128)S(1)} all-reduce(f32[32]{0:T(128)S(1)} %get-tuple-element.20), channel_id=1, replica_groups=mesh['groups'=2,'blk'=16] {'blk'}, use_global_device_ids=true, to_apply=%region_1.0 | all-reduce | flops 32 | bytes 256 | tf_op jit(solution)/shard_map/psum | solution.py:40
  113.8 8.8 %convolution_convert_fusion.6 = bf16[32,32,512]{2,1,0:T(8,128)(2,1)S(1)} fusion(bf16[32,512,512]{2,1,0:T(8,128)(2,1)} %param.11, f32[32,32,512]{2,1,0:T(8,128)S(1)} %get-tuple-element.21, f32[32]{0:T(128)S(1)} %psum.77, f32[32,512]{1,0:T(8,128)S(1)} %fusion.33), kind=kOutput, calls=%fused_computation.44 | convolution fusion | flops 539492352 | bytes 19988608 | tf_op jit(solution)/shard_map/rns,rsp->rnp/dot_general | solution.py:22
  122.6 6.4 copy.33
  129.1 7.4 reshape.47
  141.7 12.1 %convolution_convert_fusion.3 = bf16[32,32,512]{2,1,0:T(8,128)(2,1)} fusion(bf16[32,32,512]{2,1,0:T(8,128)(2,1)S(1)} %fusion.15, bf16[32,512,512]{2,1,0:T(8,128)(2,1)} %param.10), kind=kOutput, calls=%fused_computation.41 | convolution fusion | flops 537395200 | bytes 18874368 | tf_op jit(solution)/shard_map/pnq,prq->pnr/dot_general | solution.py:55
  153.8 7.2 copy.40
  161.0 7.4 reshape.45
  168.6 6.2 all-to-all-start.4
  174.8 6.5 reshape.48
  181.2 6.7 copy.34
  193.9 9.6 %multiply_reduce_fusion.5 = (f32[32]{0:T(128)S(1)}, f32[32,32,512]{2,1,0:T(8,128)}) fusion(f32[32,512]{1,0:T(8,128)S(1)} %fusion.34, bf16[32,512,512]{2,1,0:T(8,128)(2,1)} %param.10, bf16[512,32,32]{0,1,2:T(8,128)(2,1)S(1)} %all_to_all.105), kind=kOutput, calls=%fused_computation.36 | convolution fusion | flops 537919488 | bytes 19988608 | tf_op jit(solution)/shard_map/pnr,prq->pnq/dot_general | solution.py:36
  203.4 34.0 %psum.78 = f32[32]{0:T(128)S(1)} all-reduce(f32[32]{0:T(128)S(1)} %get-tuple-element.22), channel_id=1, replica_groups=mesh['groups'=2,'blk'=16] {'blk'}, use_global_device_ids=true, to_apply=%region_3.0 | all-reduce | flops 32 | bytes 256 | tf_op jit(solution)/shard_map/psum | solution.py:40
  237.4 10.4 %convolution_convert_fusion.5 = bf16[32,32,512]{2,1,0:T(8,128)(2,1)} fusion(bf16[32,512,512]{2,1,0:T(8,128)(2,1)} %param.11, f32[32,32,512]{2,1,0:T(8,128)} %get-tuple-element.23, f32[32]{0:T(128)S(1)} %psum.78, f32[32,512]{1,0:T(8,128)S(1)} %fusion.34), kind=kOutput, calls=%fused_computation.43 | convolution fusion | flops 539492352 | bytes 19988608 | tf_op jit(solution)/shard_map/rns,rsp->rnp/dot_general | solution.py:22
  247.8 7.2 copy.35
  255.0 7.4 reshape.49
  267.8 6.5 reshape.46
  274.3 6.7 copy.41
  281.0 6.8 all_to_all.114
  289.9 6.5 reshape.50
  296.4 6.7 copy.36
  303.1 6.8 all_to_all.109
  309.9 9.9 %multiply_reduce_fusion.4 = (f32[32]{0:T(128)S(1)}, f32[32,32,512]{2,1,0:T(8,128)}) fusion(f32[32,512]{1,0:T(8,128)S(1)} %copy-done.10, bf16[32,512,512]{2,1,0:T(8,128)(2,1)} %param.10, bf16[512,32,32]{0,1,2:T(8,128)(2,1)} %all_to_all.109), kind=kOutput, calls=%fused_computation.35 | convolution fusion | flops 537919488 | bytes 19988608 | tf_op jit(solution)/shard_map/pnr,prq->pnq/dot_general | solution.py:36
  319.9 34.8 %psum.79 = f32[32]{0:T(128)S(1)} all-reduce(f32[32]{0:T(128)S(1)} %get-tuple-element.24), channel_id=1, replica_groups=mesh['groups'=2,'blk'=16] {'blk'}, use_global_device_ids=true, to_apply=%region_5.0 | all-reduce | flops 32 | bytes 256 | tf_op jit(solution)/shard_map/psum | solution.py:40
  354.7 13.1 %multiply_reduce_fusion.3 = (f32[32]{0:T(128)S(1)}, f32[32]{0:T(128)S(1)}, f32[32,32,512]{2,1,0:T(8,128)}) fusion(f32[32]{0:T(128)S(1)} %psum.79, f32[32,32,512]{2,1,0:T(8,128)} %get-tuple-element.25, f32[32,512]{1,0:T(8,128)S(1)} %copy-done.10, bf16[32,512,512]{2,1,0:T(8,128)(2,1)} %param.11, bf16[512,32,32]{0,1,2:T(8,128)(2,1)} %all_to_all.114), kind=kOutput, calls=%fused_computation.31 | convolution fusion | flops 541065216 | bytes 22086016 | tf_op jit(solution)/shard_map/rnp,rsp->rns/dot_general | solution.py:63
  367.7 29.9 %psum.81 = f32[32]{0:T(128)S(1)} all-reduce(f32[32]{0:T(128)S(1)} %get-tuple-element.6), channel_id=1, replica_groups=mesh['groups'=2,'blk'=16] {'blk'}, use_global_device_ids=true, to_apply=%region_9.0 | all-reduce | flops 32 | bytes 256 | tf_op jit(solution)/shard_map/psum | solution.py:66
  400.6 12.0 %convolution_convert_fusion.2 = bf16[32,32,512]{2,1,0:T(8,128)(2,1)} fusion(bf16[32,32,512]{2,1,0:T(8,128)(2,1)} %multiply_convert_fusion.3, bf16[32,512,512]{2,1,0:T(8,128)(2,1)} %param.10), kind=kOutput, calls=%fused_computation.40 | convolution fusion | flops 537395200 | bytes 18874368 | tf_op jit(solution)/shard_map/pnq,prq->pnr/dot_general | solution.py:55
  412.6 7.2 copy.42
  419.8 7.4 reshape.51
  427.3 29.1 %all_to_all.135 = bf16[16,2,16384]{2,1,0:T(2,128)(2,1)} all-to-all(bf16[16,2,16384]{2,1,0:T(2,128)(2,1)} %reshape.51), channel_id=1, replica_groups=mesh['groups'=2,'blk'=16] {'blk'}, dimensions={0} | all-to-all | bytes 2097152 | tf_op jit(solution)/shard_map/all_to_all | solution.py:61
  456.4 6.5 reshape.52
  462.9 6.7 copy.43
  469.6 6.8 all_to_all.118
  476.4 13.6 %multiply_reduce_fusion.2 = (f32[32]{0:T(128)}, f32[32]{0:T(128)S(1)}, f32[32,32,512]{2,1,0:T(8,128)}) fusion(f32[32]{0:T(128)S(1)} %psum.78, f32[32,32,512]{2,1,0:T(8,128)} %get-tuple-element.23, f32[32,512]{1,0:T(8,128)S(1)} %fusion.34, bf16[32,512,512]{2,1,0:T(8,128)(2,1)} %param.11, bf16[512,32,32]{0,1,2:T(8,128)(2,1)} %all_to_all.118), kind=kOutput, calls=%fused_computation.27 | convolution fusion | flops 541065216 | bytes 22086016 | tf_op jit(solution)/shard_map/rnp,rsp->rns/dot_general | solution.py:63
  489.9 33.1 %psum.83 = f32[32]{0:T(128)S(1)} all-reduce(f32[32]{0:T(128)S(1)} %get-tuple-element.8), channel_id=1, replica_groups=mesh['groups'=2,'blk'=16] {'blk'}, use_global_device_ids=true, to_apply=%region_13.0 | all-reduce | flops 32 | bytes 256 | tf_op jit(solution)/shard_map/psum | solution.py:66
  526.0 12.0 %convolution_convert_fusion.1 = bf16[32,32,512]{2,1,0:T(8,128)(2,1)} fusion(bf16[32,32,512]{2,1,0:T(8,128)(2,1)} %multiply_convert_fusion.2, bf16[32,512,512]{2,1,0:T(8,128)(2,1)} %param.10), kind=kOutput, calls=%fused_computation.39 | convolution fusion | flops 537395200 | bytes 18874368 | tf_op jit(solution)/shard_map/pnq,prq->pnr/dot_general | solution.py:55
  538.1 7.2 copy.44
  545.3 7.4 reshape.53
  557.0 10.5 %convolution_convert_fusion.4 = bf16[32,32,512]{2,1,0:T(8,128)(2,1)} fusion(bf16[32,512,512]{2,1,0:T(8,128)(2,1)} %param.11, f32[32,32,512]{2,1,0:T(8,128)} %get-tuple-element.25, f32[32]{0:T(128)S(1)} %psum.79, f32[32,512]{1,0:T(8,128)S(1)} %copy-done.10), kind=kOutput, calls=%fused_computation.42 | convolution fusion | flops 539492352 | bytes 19988608 | tf_op jit(solution)/shard_map/rns,rsp->rnp/dot_general | solution.py:22
  567.5 7.2 copy.37
  574.7 7.4 reshape.57
  582.2 6.2 all-to-all-start.3
  588.4 6.5 reshape.54
  594.8 6.7 copy.45
  601.5 6.8 all_to_all.122
  608.3 12.5 %multiply_reduce_fusion.1 = (f32[32]{0:T(128)S(1)}, f32[32]{0:T(128)S(1)}, f32[32,32,512]{2,1,0:T(8,128)}) fusion(f32[32]{0:T(128)S(1)} %psum.77, f32[32,32,512]{2,1,0:T(8,128)S(1)} %get-tuple-element.21, f32[32,512]{1,0:T(8,128)S(1)} %fusion.33, bf16[32,512,512]{2,1,0:T(8,128)(2,1)} %param.11, bf16[512,32,32]{0,1,2:T(8,128)(2,1)} %all_to_all.122), kind=kOutput, calls=%fused_computation.23 | convolution fusion | flops 541065216 | bytes 22086016 | tf_op jit(solution)/shard_map/rnp,rsp->rns/dot_general | solution.py:63
  620.8 34.0 %psum.85 = f32[32]{0:T(128)S(1)} all-reduce(f32[32]{0:T(128)S(1)} %get-tuple-element.10), channel_id=1, replica_groups=mesh['groups'=2,'blk'=16] {'blk'}, use_global_device_ids=true, to_apply=%region_17.0 | all-reduce | flops 32 | bytes 256 | tf_op jit(solution)/shard_map/psum | solution.py:66
  656.8 11.1 %convolution_convert_fusion = bf16[32,32,512]{2,1,0:T(8,128)(2,1)S(1)} fusion(bf16[32,32,512]{2,1,0:T(8,128)(2,1)S(1)} %multiply_convert_fusion.1, bf16[32,512,512]{2,1,0:T(8,128)(2,1)} %param.10), kind=kOutput, calls=%fused_computation.38 | convolution fusion | flops 537395200 | bytes 18874368 | tf_op jit(solution)/shard_map/pnq,prq->pnr/dot_general | solution.py:55
  667.9 6.4 copy.46
  674.3 7.4 reshape.55
  686.3 6.5 reshape.58
  692.8 7.1 copy.38
  699.8 7.3 reshape.40
  712.0 6.7 copy.47
  718.7 6.0 all_to_all.126
  724.8 12.2 %fusion.42 = (f32[32]{0:T(128)S(1)}, f32[32]{0:T(128)S(1)}, f32[32,32,512]{2,1,0:T(8,128)}) fusion(bf16[4,32,8,512]{3,2,1,0:T(8,128)(2,1)S(1)} %bitcast.192, bf16[32,512,512]{2,1,0:T(8,128)(2,1)} %param.11, bf16[512,32,32]{0,1,2:T(8,128)(2,1)S(1)} %all_to_all.126), kind=kOutput, calls=%fused_computation.86 | convolution fusion | flops 538968064 | bytes 20971776 | tf_op jit(solution)/shard_map/rnp,rsp->rns/dot_general | solution.py:63
  736.9 34.8 %all-reduce = (f32[32]{0:T(128)S(1)}, f32[32]{0:T(128)S(1)}, f32[32]{0:T(128)S(1)}, f32[32]{0:T(128)S(1)}, f32[32]{0:T(128)S(1)}) all-reduce(f32[32]{0:T(128)S(1)} %get-tuple-element.4, f32[32]{0:T(128)S(1)} %get-tuple-element.9, f32[32]{0:T(128)S(1)} %copy-done.12, ...), channel_id=1, replica_groups=mesh['groups'=2,'blk'=16] {'blk'}, use_global_device_ids=true, to_apply=%region_19.0 | all-reduce | flops 160 | bytes 1280 | tf_op jit(solution)/shard_map/psum | solution.py:66
  780.0 16.9 %multiply_convert_fusion = bf16[32,512,512]{2,1,0:T(8,128)(2,1)} fusion(bf16[32,512,512]{2,1,0:T(8,128)(2,1)} %param.10, bf16[32,32,512]{2,1,0:T(8,128)(2,1)} %get-tuple-element.30, bf16[32,32,512]{2,1,0:T(8,128)(2,1)} %get-tuple-element.31, bf16[32,32,512]{2,1,0:T(8,128)(2,1)} %divide_convert_fusion.5, bf16[32,32,512]{2,1,0:T(8,128)(2,1)} %fusion.30, ...), kind=kOutput, calls=%fused_computation | convolution fusion | flops 2214592512 | bytes 41943040 | tf_op jit(solution)/shard_map/pnr,pnq->prq/dot_general | solution.py:78
  (61 shorter events, 58.3 us)
Async XLA Ops:
  0.6 30.2 %copy-start = (bf16[256,512]{1,0:T(8,128)(2,1)S(1)}, bf16[256,512]{1,0:T(8,128)(2,1)}, u32[]{:S(2)}) copy-start(bf16[256,512]{1,0:T(8,128)(2,1)} %param.9) | copy-start | bytes 786436
  23.3 7.5 copy-start.13
  23.3 30.5 %all-to-all-start = ((bf16[16,2,16384]{2,1,0:T(2,128)(2,1)}), bf16[16,2,16384]{2,1,0:T(2,128)(2,1)S(1)}, u32[]{:S(2)}, u32[]{:S(2)}) async-start(bf16[16,2,16384]{2,1,0:T(2,128)(2,1)} %reshape.43), calls=%async_computation | async-start | bytes 2097152 | tf_op jit(solution)/shard_map/all_to_all | solution.py:31
  69.9 8.6 %copy-start.2 = (bf16[512,32,32]{0,1,2:T(8,128)(2,1)}, bf16[512,32,32]{0,1,2:T(8,128)(2,1)S(1)}, u32[]{:S(2)}) copy-start(bf16[512,32,32]{0,1,2:T(8,128)(2,1)S(1)} %all_to_all.101) | copy-start | bytes 3145732
  136.5 4.5 copy-start.11
  136.5 32.1 %all-to-all-start.1 = ((bf16[16,2,16384]{2,1,0:T(2,128)(2,1)}), bf16[16,2,16384]{2,1,0:T(2,128)(2,1)}, u32[]{:S(2)}, u32[]{:S(2)}) async-start(bf16[16,2,16384]{2,1,0:T(2,128)(2,1)} %reshape.47), calls=%async_computation.1 | async-start | bytes 2097152 | tf_op jit(solution)/shard_map/all_to_all | solution.py:31
  141.7 12.1 %copy-start.7 = (bf16[32,32,512]{2,1,0:T(8,128)(2,1)}, bf16[32,32,512]{2,1,0:T(8,128)(2,1)S(1)}, u32[]{:S(2)}) copy-start(bf16[32,32,512]{2,1,0:T(8,128)(2,1)S(1)} %fusion.15) | copy-start | bytes 3145732
  168.6 93.9 %all-to-all-start.4 = ((bf16[16,2,16384]{2,1,0:T(2,128)(2,1)}), bf16[16,2,16384]{2,1,0:T(2,128)(2,1)}, u32[]{:S(2)}, u32[]{:S(2)}) async-start(bf16[16,2,16384]{2,1,0:T(2,128)(2,1)} %reshape.45), calls=%async_computation.4 | async-start | bytes 2097152 | tf_op jit(solution)/shard_map/all_to_all | solution.py:59
  262.4 27.5 %all-to-all-start.2 = ((bf16[16,2,16384]{2,1,0:T(2,128)(2,1)}), bf16[16,2,16384]{2,1,0:T(2,128)(2,1)}, u32[]{:S(2)}, u32[]{:S(2)}) async-start(bf16[16,2,16384]{2,1,0:T(2,128)(2,1)} %reshape.49), calls=%async_computation.2 | async-start | bytes 2097152 | tf_op jit(solution)/shard_map/all_to_all | solution.py:31
  303.1 6.8 copy-start.10
  552.7 29.5 %all-to-all-start.6 = ((bf16[16,2,16384]{2,1,0:T(2,128)(2,1)}), bf16[16,2,16384]{2,1,0:T(2,128)(2,1)}, u32[]{:S(2)}, u32[]{:S(2)}) async-start(bf16[16,2,16384]{2,1,0:T(2,128)(2,1)} %reshape.53), calls=%async_computation.6 | async-start | bytes 2097152 | tf_op jit(solution)/shard_map/all_to_all | solution.py:61
  582.2 99.6 %all-to-all-start.3 = ((bf16[16,2,16384]{2,1,0:T(2,128)(2,1)}), bf16[16,2,16384]{2,1,0:T(2,128)(2,1)}, u32[]{:S(2)}, u32[]{:S(2)}) async-start(bf16[16,2,16384]{2,1,0:T(2,128)(2,1)} %reshape.57), calls=%async_computation.3 | async-start | bytes 2097152 | tf_op jit(solution)/shard_map/all_to_all | solution.py:47
  656.7 11.1 %copy-start.9 = (bf16[32,32,512]{2,1,0:T(8,128)(2,1)}, bf16[32,32,512]{2,1,0:T(8,128)(2,1)S(1)}, u32[]{:S(2)}) copy-start(bf16[32,32,512]{2,1,0:T(8,128)(2,1)S(1)} %multiply_convert_fusion.1) | copy-start | bytes 3145732
  681.8 26.8 %all-to-all-start.7 = ((bf16[16,2,16384]{2,1,0:T(2,128)(2,1)}), bf16[16,2,16384]{2,1,0:T(2,128)(2,1)S(1)}, u32[]{:S(2)}, u32[]{:S(2)}) async-start(bf16[16,2,16384]{2,1,0:T(2,128)(2,1)} %reshape.55), calls=%async_computation.7 | async-start | bytes 2097152 | tf_op jit(solution)/shard_map/all_to_all | solution.py:61
  718.7 6.0 copy-start.6
  724.8 12.2 %copy-start.12 = (f32[32]{0:T(128)S(1)}, f32[32]{0:T(128)}, u32[]{:S(2)}) copy-start(f32[32]{0:T(128)} %get-tuple-element.7) | copy-start | bytes 388
  771.8 3.4 copy-start.4
  774.1 2.5 copy-start.5
  776.6 1.3 copy-start.3
  777.9 2.1 copy-start.8
  780.0 16.9 %copy-start.1 = (bf16[256,512]{1,0:T(8,128)(2,1)S(1)}, bf16[256,512]{1,0:T(8,128)(2,1)}, u32[]{:S(2)}) copy-start(bf16[256,512]{1,0:T(8,128)(2,1)} %param.9) | copy-start | bytes 786436
where the time goes:
time: 808 us; the launch traced here: 797 us
  local copies, waits for them, and re-layouts  268 us (33%)
  blocking collectives  265 us (33%)
  matrix products  183 us (23%)
  starting transfers between devices  37.1 us (5%)
  waiting for transfers between devices  26.3 us (3%)
  other arithmetic  16.2 us (2%)
    psum x4, blocking collectives, on_device(): lax.psum((jnp.sum(prior, axis=(0, 2)), jnp.sum(forwards[step - 1] * prior...  132 us
    unnamed x44, local copies, waits for them, and re-layouts  105 us
    psum x3, blocking collectives, on_device(): forward_total = lax.psum(jnp.sum(weighted, axis=(0, 2)), 'blk')  104 us
    all_to_all x8, local copies, waits for them, and re-layouts, on_device(): lax.all_to_all(back_sums, 'blk', split_axis=2, concat_axis=0, tiled=True)  53.2 us
    dot_general x4, matrix products, on_device(): jnp.einsum('rnp,rsp->rns', turned_back, right_factor, preferred_element_t...  51.3 us
    dot_general x4, matrix products, on_device(): jnp.einsum('pnq,prq->pnr', emitted, left_factor, preferred_element_type=j...  47.3 us
    all_to_all x6, local copies, waits for them, and re-layouts, on_device(): lax.all_to_all(path_sums(forward_msg), 'blk', split_axis=2, concat_axis=0...  38.8 us
    dot_general x4, matrix products, path_sums(): jnp.einsum('rns,rsp->rnp', message, right_factor, preferred_element_type=...  38.5 us
  transfers between devices with their start and end apart: 7, of which 3 were waited for; matrix products, arithmetic and copies ran while one was open for 24% of the time, Pallas kernels for 0%

commit v1 on v0

--- a/solution.py
+++ b/solution.py
@@ -1,7 +1,492 @@
+import functools
+
 import jax
 import jax.numpy as jnp
 from jax import lax
+from jax.experimental import pallas as pl
+from jax.experimental.pallas import tpu as pltpu
 from jax.sharding import PartitionSpec as P
+
+LANES = 128
+SUBLANES = 8
+MIB = 1 << 20
+
+
+def dot(x, w, w_dim):
+    return lax.dot_general(
+        x, w, (((1,), (w_dim,)), ((), ())), preferred_element_type=jnp.float32
+    )
+
+
+def messages_kernel(
+    devices,
+    window,
+    alpha_hbm,
+    beta_hbm,
+    left_hbm,
+    right_hbm,
+    rows_ref,
+    paths_hbm,
+    values_hbm,
+    beta_out_hbm,
+    totals_ref,
+    post_ref,
+    mean_ref,
+    left,
+    right,
+    alpha_first,
+    alphas,
+    beta_flat,
+    prior_last_step,
+    values,
+    paths,
+    staged,
+    unpacked,
+    outbox,
+    inbox,
+    small_out,
+    small_in,
+    post_sums,
+    left_sem,
+    right_sem,
+    message_sem,
+    out_sem,
+    own_sem,
+    send_sem,
+    recv_sem,
+    small_send_sem,
+    small_recv_sem,
+):
+    blocks, size, _ = left.shape
+    seqs = alpha_first.shape[0]
+    states = size * size
+    tiles = size // LANES
+    group = LANES // blocks
+    steps = window - 1
+    chunks = left_sem.shape[0]
+    per_chunk = blocks // chunks
+    me = lax.axis_index("blk")
+
+    def loop(count, body, start=0, unroll=1):
+        def wrapped(i, carry):
+            body(i)
+            return carry
+
+        lax.fori_loop(start, count, wrapped, 0, unroll=unroll)
+
+    def chunk_copy(hbm, ref, sem, c):
+        part = pl.ds(c * per_chunk, per_chunk)
+        return pltpu.make_async_copy(hbm.at[part], ref.at[part], sem.at[c])
+
+    alpha_copy = pltpu.make_async_copy(alpha_hbm, alpha_first, message_sem.at[0])
+    beta_copy = pltpu.make_async_copy(beta_hbm, beta_flat, message_sem.at[1])
+    alpha_copy.start()
+    loop(chunks, lambda c: chunk_copy(right_hbm, right, right_sem, c).start())
+    beta_copy.start()
+    loop(chunks, lambda c: chunk_copy(left_hbm, left, left_sem, c).start())
+
+    barrier = pltpu.get_barrier_semaphore()
+
+    def greet(off):
+        pl.semaphore_signal(
+            barrier,
+            inc=1,
+            device_id={"blk": lax.rem(me + off, devices)},
+            device_id_type=pl.DeviceIdType.MESH,
+        )
+
+    loop(devices, greet, 1)
+    pl.semaphore_wait(barrier, devices - 1)
+
+    def block_copy(chain, par, off, landing):
+        other = lax.rem(me + off, devices)
+        return pltpu.make_async_remote_copy(
+            src_ref=outbox.at[chain, pl.ds(pl.multiple_of(other * blocks, blocks), blocks)],
+            dst_ref=inbox.at[chain, par, landing(other)],
+            send_sem=send_sem.at[chain, off],
+            recv_sem=recv_sem.at[chain, par, landing(other)],
+            device_id={"blk": other},
+            device_id_type=pl.DeviceIdType.MESH,
+        )
+
+    def own_copy(chain, par):
+        return pltpu.make_async_copy(
+            outbox.at[chain, pl.ds(pl.multiple_of(me * blocks, blocks), blocks)],
+            inbox.at[chain, par, me],
+            own_sem.at[chain],
+        )
+
+    def sent(chain, par):
+        loop(devices, lambda off: block_copy(chain, par, off, lambda other: me).wait_send(), 1)
+
+    def pack_and_send(chain, par):
+        def pack(j):
+            lanes = pl.ds(pl.multiple_of(j * LANES, LANES), LANES)
+            for k in range(tiles):
+                picked = [
+                    staged[k, pl.ds(j * group + c, blocks, stride=seqs), :] for c in range(group)
+                ]
+                turned = jnp.transpose(jnp.concatenate(picked, axis=0))
+                outbox[chain, k * LANES : (k + 1) * LANES, lanes] = turned.astype(jnp.bfloat16)
+
+        loop(seqs // group, pack)
+        loop(devices, lambda off: block_copy(chain, par, off, lambda other: me).start(), 1)
+        own_copy(chain, par).start()
+
+    def receive(chain, par):
+        own_copy(chain, par).wait()
+        loop(devices, lambda off: block_copy(chain, par, off, lambda other: other).wait_recv(), 1)
+        place = lax.broadcasted_iota(jnp.int32, (blocks, LANES), 1) // blocks
+
+        def merge(pieces):
+            merged = pieces[0]
+            for g in range(1, group):
+                merged = jnp.where(place == g, pieces[g], merged)
+            return merged
+
+        def unpack(j):
+            lanes = pl.ds(pl.multiple_of(j * LANES, LANES), LANES)
+            for k in range(tiles):
+                came = [
+                    inbox[chain, par, k * group + i, :, lanes].astype(jnp.float32)
+                    for i in range(group)
+                ]
+                shifted = []
+                for s in range(group):
+                    mixed = merge([came[(g + s) % group] for g in range(group)])
+                    shifted.append(pltpu.roll(mixed, s * blocks, 1) if s else mixed)
+                for c in range(group):
+                    unpacked[k, pl.ds(j * group + c, blocks, stride=seqs), :] = merge(
+                        [shifted[(i - c) % group] for i in range(group)]
+                    )
+
+        loop(seqs // group, unpack)
+
+    def small_copy(kind, slot, off, landing):
+        other = lax.rem(me + off, devices)
+        return pltpu.make_async_remote_copy(
+            src_ref=small_out.at[kind],
+            dst_ref=small_in.at[slot, landing(other)],
+            send_sem=small_send_sem.at[kind, off],
+            recv_sem=small_recv_sem.at[slot, landing(other)],
+            device_id={"blk": other},
+            device_id_type=pl.DeviceIdType.MESH,
+        )
+
+    def small_sent(kind, slot):
+        loop(devices, lambda off: small_copy(kind, slot, off, lambda other: me).wait_send(), 1)
+
+    def small_send(kind, slot, columns):
+        lane = lax.broadcasted_iota(jnp.int32, (SUBLANES, LANES), 1)
+        tile = jnp.zeros((SUBLANES, LANES), jnp.float32)
+        for c, column in enumerate(columns):
+            for i in range(seqs // SUBLANES):
+                part = column[i * SUBLANES : (i + 1) * SUBLANES, :]
+                tile = jnp.where(lane == c * (seqs // SUBLANES) + i, part, tile)
+        small_out[kind] = tile
+        small_in[slot, me] = tile
+        loop(devices, lambda off: small_copy(kind, slot, off, lambda other: me).start(), 1)
+
+    def small_receive(kind, slot, count):
+        loop(devices, lambda off: small_copy(kind, slot, off, lambda other: other).wait_recv(), 1)
+        total = jnp.sum(small_in[slot], axis=0)
+        per = seqs // SUBLANES
+        return [
+            jnp.concatenate(
+                [total[:, c * per + i : c * per + i + 1] for i in range(per)], axis=0
+            )
+            for c in range(count)
+        ]
+
+    def flat(b):
+        return pl.ds(pl.multiple_of(b * size, size), size)
+
+    def block_rows(b):
+        return pl.ds(pl.multiple_of(b * seqs, seqs), seqs)
+
+    def stage(b, result):
+        for k in range(tiles):
+            staged[k, block_rows(b), :] = result[:, k * LANES : (k + 1) * LANES]
+
+    def arrived(b):
+        return jnp.concatenate(
+            [unpacked[k, block_rows(b), :] for k in range(tiles)], axis=1
+        ).astype(jnp.bfloat16)
+
+    def narrow(wide):
+        total = wide[:, :LANES]
+        for k in range(1, tiles):
+            total = total + wide[:, k * LANES : (k + 1) * LANES]
+        return total
+
+    zero = jnp.zeros((seqs, LANES), jnp.float32)
+
+    def column(total):
+        return jnp.sum(total, axis=1, keepdims=True)
+
+    alpha_copy.wait()
+
+    def first_path(c):
+        chunk_copy(right_hbm, right, right_sem, c).wait()
+        loop(
+            per_chunk,
+            lambda i: stage(
+                c * per_chunk + i,
+                dot(alpha_first[:, flat(c * per_chunk + i)], right[c * per_chunk + i], 0),
+            ),
+        )
+
+    loop(chunks, first_path)
+    pack_and_send(0, 0)
+    even = jnp.full((seqs, 1), states / devices, jnp.float32)
+    small_send(0, 0, [even])
+
+    beta_copy.wait()
+
+    def first_back(c):
+        chunk_copy(left_hbm, left, left_sem, c).wait()
+
+        def one(i):
+            b = c * per_chunk + i
+            emitted = rows_ref[steps].astype(jnp.float32) * beta_flat[:, flat(b)].astype(
+                jnp.float32
+            )
+            values[steps, b] = emitted.astype(jnp.bfloat16)
+            stage(b, dot(values[steps, b], left[b], 1))
+
+        loop(per_chunk, one)
+
+    loop(chunks, first_back)
+    pack_and_send(1, 0)
+    small_send(1, 2, [even])
+
+    def values_copy(t):
+        return pltpu.make_async_copy(values.at[t], values_hbm.at[:, t], out_sem.at[0, t])
+
+    def paths_copy(t):
+        return pltpu.make_async_copy(paths.at[t], paths_hbm.at[:, t], out_sem.at[1, t])
+
+    values_copy(steps).start()
+
+    def keep_mean(ref, index, total):
+        mean = total * (1.0 / states)
+        ref[index] = jnp.broadcast_to(mean, (seqs, LANES))
+        return 1.0 / mean
+
+    def step_body(k):
+        par, later = lax.rem(k, 2), lax.rem(k + 1, 2)
+
+        receive(0, par)
+        (total,) = small_receive(0, par, 1)
+        scale = keep_mean(totals_ref, k, total)
+
+        def forward(b, acc):
+            path = arrived(b)
+            paths[k, b] = path
+            ahead = dot(path, left[b], 0)
+            weighted = ahead * (rows_ref[k].astype(jnp.float32) * scale)
+            alphas[k, b] = weighted.astype(jnp.bfloat16)
+            return acc + narrow(weighted)
+
+        acc = lax.fori_loop(0, blocks, forward, zero, unroll=2)
+        small_sent(0, par)
+        small_send(0, later, [column(acc)])
+        paths_copy(k).start()
+        loop(blocks, lambda b: stage(b, dot(alphas[k, b], right[b], 0)), unroll=2)
+        sent(0, par)
+        pack_and_send(0, later)
+
+        receive(1, par)
+        (total,) = small_receive(1, 2 + par, 1)
+        scale = keep_mean(mean_ref, steps - k, total)
+
+        def backward(b, accs):
+            prior = dot(arrived(b), right[b], 1) * scale
+            prior_last_step[lax.min(k, 1), b] = prior.astype(jnp.bfloat16)
+            emitted = rows_ref[steps - 1 - k].astype(jnp.float32) * prior
+            values[steps - 1 - k, b] = emitted.astype(jnp.bfloat16)
+            both = alphas[post_source(k), b].astype(jnp.float32) * prior
+            return accs[0] + narrow(prior), accs[1] + narrow(both)
+
+        acc, post = lax.fori_loop(0, blocks, backward, (zero, zero), unroll=2)
+        small_sent(1, 2 + par)
+        small_send(1, 2 + later, [column(acc)])
+        post_sums[steps - k] = post
+        values_copy(steps - 1 - k).start()
+        loop(
+            blocks,
+            lambda b: stage(b, dot(values[steps - 1 - k, b], left[b], 1)),
+            unroll=2,
+        )
+        sent(1, par)
+        pack_and_send(1, later)
+
+    def post_source(k):
+        return lax.min(steps - 1 - k, k)
+
+    loop(steps, step_body)
+    par = steps % 2
+
+    for late in range(steps):
+        if steps - 1 - late > late:
+
+            def late_post(b, acc):
+                both = alphas[steps - 1 - late, b].astype(jnp.float32) * prior_last_step[
+                    late, b
+                ].astype(jnp.float32)
+                return acc + narrow(both)
+
+            post_sums[steps - late] = lax.fori_loop(0, blocks, late_post, zero)
+
+    receive(0, par)
+    (total,) = small_receive(0, par, 1)
+    keep_mean(totals_ref, steps, total)
+
+    def last_path(b):
+        paths[steps, b] = arrived(b)
+
+    loop(blocks, last_path)
+    paths_copy(steps).start()
+
+    receive(1, par)
+    (total,) = small_receive(1, 2 + par, 1)
+    scale = keep_mean(mean_ref, 0, total)
+
+    def last_prior(b, accs):
+        prior = dot(arrived(b), right[b], 1) * scale
+        stage(b, prior)
+        both = alpha_first[:, flat(b)].astype(jnp.float32) * prior
+        return accs[0] + narrow(prior), accs[1] + narrow(both)
+
+    acc, post = lax.fori_loop(0, blocks, last_prior, (zero, zero), unroll=2)
+    post_sums[0] = post
+    small_send(2, 4, [column(acc)] + [column(post_sums[t]) for t in range(window)])
+    found = small_receive(2, 4, 1 + window)
+    norm = states / found[0]
+    for t in range(window):
+        post_ref[t] = jnp.broadcast_to(found[1 + t], (seqs, LANES))
+
+    def last_beta(b):
+        wide = jnp.concatenate([staged[k, block_rows(b), :] for k in range(tiles)], axis=1)
+        beta_flat[:, flat(b)] = (wide * norm).astype(jnp.bfloat16)
+
+    loop(blocks, last_beta)
+    result = pltpu.make_async_copy(beta_flat, beta_out_hbm, message_sem.at[0])
+    result.start()
+    for t in range(window):
+        values_copy(t).wait()
+        paths_copy(t).wait()
+    sent(0, par)
+    sent(1, par)
+    small_sent(0, par)
+    small_sent(1, 2 + par)
+    small_sent(2, 4)
+    result.wait()
+
+
+def counts_kernel(factor, post_ref, mean_ref, left_ref, paths_ref, values_ref, count_ref):
+    for i in range(left_ref.shape[0]):
+        scaled = paths_ref[i].astype(jnp.float32) / post_ref[:, :1] / mean_ref[:, :1]
+        tally = lax.dot_general(
+            scaled.astype(jnp.bfloat16),
+            values_ref[i],
+            (((0,), (0,)), ((), ())),
+            preferred_element_type=jnp.float32,
+        )
+        count_ref[i] = (left_ref[i].astype(jnp.float32) * tally * factor).astype(jnp.bfloat16)
+
+
+def on_device_fused(devices, tokens, alpha_start, beta_in, emission, left_factor, right_factor):
+    blocks, size, _ = left_factor.shape
+    seqs = alpha_start.shape[0]
+    window = tokens.shape[0]
+    vocab = emission.shape[0]
+    steps = window - 1
+    picked = tokens.reshape(-1)[:, None] == lax.broadcasted_iota(
+        jnp.int32, (window * seqs, vocab), 1
+    )
+    rows = jnp.dot(
+        picked.astype(jnp.bfloat16), emission, preferred_element_type=jnp.float32
+    ).reshape(window, seqs, size)
+    any_space = pl.BlockSpec(memory_space=pl.ANY)
+    in_vmem = pl.BlockSpec(memory_space=pltpu.VMEM)
+    bf16, f32 = jnp.bfloat16, jnp.float32
+    tiles = size // LANES
+    chunks = 4
+    per_step = jax.ShapeDtypeStruct((window, seqs, LANES), f32)
+    kept = jax.ShapeDtypeStruct((blocks, window, seqs, size), bf16)
+    messages = (blocks, seqs, size)
+    turned = (tiles, blocks * seqs, LANES)
+    paths, values, beta_out, totals, post, mean = pl.pallas_call(
+        functools.partial(messages_kernel, devices, window),
+        out_shape=(
+            kept,
+            kept,
+            jax.ShapeDtypeStruct(beta_in.shape, bf16),
+            per_step,
+            per_step,
+            per_step,
+        ),
+        in_specs=[any_space] * 4 + [in_vmem],
+        out_specs=(any_space,) * 3 + (in_vmem,) * 3,
+        scratch_shapes=[
+            pltpu.VMEM(left_factor.shape, bf16),
+            pltpu.VMEM(right_factor.shape, bf16),
+            pltpu.VMEM(alpha_start.shape, bf16),
+            pltpu.VMEM((steps,) + messages, bf16),
+            pltpu.VMEM(beta_in.shape, bf16),
+            pltpu.VMEM((2,) + messages, bf16),
+            pltpu.VMEM((window,) + messages, bf16),
+            pltpu.VMEM((window,) + messages, bf16),
+            pltpu.VMEM(turned, f32),
+            pltpu.VMEM(turned, f32),
+            pltpu.VMEM((2, size, seqs * blocks), bf16),
+            pltpu.VMEM((2, 2, devices, blocks, seqs * blocks), bf16),
+            pltpu.VMEM((3, SUBLANES, LANES), f32),
+            pltpu.VMEM((5, devices, SUBLANES, LANES), f32),
+            pltpu.VMEM((window, seqs, LANES), f32),
+            pltpu.SemaphoreType.DMA((chunks,)),
+            pltpu.SemaphoreType.DMA((chunks,)),
+            pltpu.SemaphoreType.DMA((2,)),
+            pltpu.SemaphoreType.DMA((2, window)),
+            pltpu.SemaphoreType.DMA((2,)),
+            pltpu.SemaphoreType.DMA((2, devices)),
+            pltpu.SemaphoreType.DMA((2, 2, devices)),
+            pltpu.SemaphoreType.DMA((3, devices)),
+            pltpu.SemaphoreType.DMA((5, devices)),
+        ],
+        compiler_params=pltpu.CompilerParams(
+            collective_id=0, has_side_effects=True, vmem_limit_bytes=62 * MIB
+        ),
+    )(alpha_start, beta_in, left_factor, right_factor, rows)
+    per_call = 2
+    rows_all = window * seqs
+    factor = size * (size * size / seqs)
+    scale_spec = pl.BlockSpec((rows_all, LANES), lambda b: (0, 0))
+    factor_spec = pl.BlockSpec((per_call, size, size), lambda b: (b, 0, 0))
+    kept_spec = pl.BlockSpec((per_call, rows_all, size), lambda b: (b, 0, 0))
+    count_left = pl.pallas_call(
+        functools.partial(counts_kernel, factor),
+        grid=(blocks // per_call,),
+        out_shape=jax.ShapeDtypeStruct(left_factor.shape, bf16),
+        in_specs=[scale_spec, scale_spec, factor_spec, kept_spec, kept_spec],
+        out_specs=factor_spec,
+        compiler_params=pltpu.CompilerParams(vmem_limit_bytes=32 * MIB),
+    )(
+        post.reshape(rows_all, LANES),
+        mean.reshape(rows_all, LANES),
+        left_factor,
+        paths.reshape(blocks, rows_all, size),
+        values.reshape(blocks, rows_all, size),
+    )
+    log_scales = jnp.log(totals[1:, :, 0])
+    return count_left, beta_out, log_scales
+
+
+def fused_fits(seqs, blocks, size):
+    if blocks % 16 or LANES % blocks or size % LANES or seqs % 16:
+        return False
+    return seqs % (LANES // blocks) == 0
 
 
 def on_device(tokens, alpha_start, beta_in, emission, left_factor, right_factor):
@@ -94,6 +579,13 @@
         P("blk", None, None),
     )
     out_specs = (P(("groups", "blk"), None, None), P("groups", "blk"), P(None, "groups"))
+    devices = mesh.shape["blk"]
+
+    def body(*operands):
+        if fused_fits(operands[1].shape[0], *operands[4].shape[:2]):
+            return on_device_fused(devices, *operands)
+        return on_device(*operands)
+
     return jax.shard_map(
-        on_device, mesh=mesh, in_specs=in_specs, out_specs=out_specs, check_vma=False
-    )
+        body, mesh=mesh, in_specs=in_specs, out_specs=out_specs, check_vma=False
+    )

time: 808 us -> 272 us (0.34); the launches traced: 797 us -> 271 us
  blocking collectives: 265 us -> 0 us
  Pallas kernels: 0 us -> 260 us
  local copies, waits for them, and re-layouts: 268 us -> 9.47 us
  matrix products: 183 us -> 0.93 us
  starting transfers between devices: 37.1 us -> 0 us
  waiting for transfers between devices: 26.3 us -> 0 us
  other arithmetic: 16.2 us -> 0 us
    pallas_call x0 -> x2, Pallas kernels: none -> 260 us  [the longest x1 240 us: on_device_fused(): pl.pallas_call(functools.partial(messages_kernel, devices, window), out_s...]
    psum x7 -> x0, blocking collectives: 236 us -> none  [the longest x4 132 us: on_device(): lax.psum((jnp.sum(prior, axis=(0, 2)), jnp.sum(forwards[step - 1] * prior...]
    dot_general x20 -> x1, matrix products: 183 us -> 0.93 us  [on_device_fused(): jnp.dot(picked.astype(jnp.bfloat16), emission, preferred_element_type=jnp...]
    unnamed x44 -> x13, local copies, waits for them, and re-layouts: 105 us -> 7.18 us
    all_to_all x14 -> x0, local copies, waits for them, and re-layouts: 92 us -> none  [the longest x8 53.2 us: on_device(): lax.all_to_all(back_sums, 'blk', split_axis=2, concat_axis=0, tiled=True)]
    convert_element_type x10 -> x0, local copies, waits for them, and re-layouts: 69.7 us -> none  [the longest x4 28 us: on_device(): back_sums = jnp.einsum('pnq,prq->pnr', emitted, left_factor, preferred_el...]
    all_to_all x7 -> x0, starting transfers between devices: 37.1 us -> none  [the longest x3 16.5 us: on_device(): lax.all_to_all(path_sums(forward_msg), 'blk', split_axis=2, concat_axis=0...]
    all_to_all x1 -> x0, blocking collectives: 29.1 us -> none  [on_device(): lax.all_to_all(back_sums, 'blk', split_axis=2, concat_axis=0, tiled=True)]
  transfers between devices with their start and end apart: 7 -> 0, of which waited for: 3 -> 0; matrix products, arithmetic and copies ran while one was open for 24% -> 0% of each run, Pallas kernels for 0% -> 0%
where the time goes in v1:
time: 272 us; the launch traced here: 271 us
  Pallas kernels  260 us (96%)
  local copies, waits for them, and re-layouts  9.47 us (3%)
    pallas_call x1, Pallas kernels, on_device_fused(): pl.pallas_call(functools.partial(messages_kernel, devices, window), out_s...  240 us
    pallas_call x1, Pallas kernels, on_device_fused(): pl.pallas_call(functools.partial(counts_kernel, factor), grid=(blocks //...  20.6 us
    unnamed x13, local copies, waits for them, and re-layouts  7.18 us

profile of v1, /device:TPU:0, one launch (start us, length us, event | category | flops | bytes accessed | tf_op | source)
XLA Modules:
  0.0 271.3 jit_solution(18089813717679347354)
XLA Ops:
  0.6 0.0 copy-start
  0.6 0.8 eq.10
  1.5 0.2 copy-done
  1.6 0.9 fusion
  2.5 239.7 %shard_map.85 = (bf16[32,4,32,512]{3,2,1,0:T(8,128)(2,1)}, bf16[32,4,32,512]{3,2,1,0:T(8,128)(2,1)}, bf16[32,16384]{1,0:T(8,128)(2,1)}, f32[4,32,128]{2,1,0:T(8,...) custom-call(bf16[32,16384]{1,0:T(8,128)(2,1)} %alpha_hbm.1, bf16[32,16384]{1,0:T(8,128)(2,1)} %beta_hbm.1, ...), custom_call_target="tpu_custom_call" | custom-call | tf_op jit(solution)/shard_map/pallas_call | solution.py:420
  242.2 1.5 log_reduce_fusion
  243.7 0.0 copy-start.1
  243.7 2.2 copy-done.1
  245.9 0.0 copy-start.2
  245.9 2.2 copy-done.2
  248.1 0.0 copy-start.3
  248.1 0.8 copy-done.3
  248.9 0.0 copy-start.4
  248.9 0.8 copy-done.4
  249.8 0.0 copy-start.5
  249.8 20.6 %shard_map.86 = bf16[32,512,512]{2,1,0:T(8,128)(2,1)} custom-call(f32[128,128]{1,0:T(8,128)S(1)} %bitcast.8, f32[128,128]{1,0:T(8,128)S(1)} %bitcast.9, bf16[32,512,512]{2,1,0:T(8,128)(2,1)} %left_ref.1, bf16[32,128,512]{2,1,0:T(8,128)(2,1)S(1)} %bitcast.6, bf16[32,128,512]{2,1,0:T(8,128)(2,1)S(1)} %bitcast.7), custom_call_target="tpu_custom_call" | custom-call | tf_op jit(solution)/shard_map/pallas_call | solution.py:468
  270.4 0.0 copy-done.5
  270.4 1.0 copy.10
Async XLA Ops:
  0.6 1.0 copy-start
  243.7 2.2 copy-start.1
  245.9 2.2 copy-start.2
  248.1 0.8 copy-start.3
  248.9 0.8 copy-start.4
  249.8 20.6 %copy-start.5 = (bf16[32,16384]{1,0:T(8,128)(2,1)S(1)}, bf16[32,16384]{1,0:T(8,128)(2,1)}, u32[]{:S(2)}) copy-start(bf16[32,16384]{1,0:T(8,128)(2,1)} %get-tuple-element.19) | copy-start | bytes 3145732

commit v2 on v1

--- a/solution.py
+++ b/solution.py
@@ -130,7 +130,7 @@
                 outbox[chain, k * LANES : (k + 1) * LANES, lanes] = turned.astype(jnp.bfloat16)
 
         loop(seqs // group, pack)
-        loop(devices, lambda off: block_copy(chain, par, off, lambda other: me).start(), 1)
+        loop(devices, lambda i: block_copy(chain, par, lax.rem(i * 7, devices), lambda other: me).start(), 1)
         own_copy(chain, par).start()
 
     def receive(chain, par):
@@ -385,8 +385,9 @@
 
 
 def counts_kernel(factor, post_ref, mean_ref, left_ref, paths_ref, values_ref, count_ref):
+    over_post, over_mean = 1.0 / post_ref[:, :1], 1.0 / mean_ref[:, :1]
     for i in range(left_ref.shape[0]):
-        scaled = paths_ref[i].astype(jnp.float32) / post_ref[:, :1] / mean_ref[:, :1]
+        scaled = paths_ref[i].astype(jnp.float32) * over_post * over_mean
         tally = lax.dot_general(
             scaled.astype(jnp.bfloat16),
             values_ref[i],
@@ -459,7 +460,7 @@
             collective_id=0, has_side_effects=True, vmem_limit_bytes=62 * MIB
         ),
     )(alpha_start, beta_in, left_factor, right_factor, rows)
-    per_call = 2
+    per_call = 4
     rows_all = window * seqs
     factor = size * (size * size / seqs)
     scale_spec = pl.BlockSpec((rows_all, LANES), lambda b: (0, 0))
@@ -471,7 +472,7 @@
         out_shape=jax.ShapeDtypeStruct(left_factor.shape, bf16),
         in_specs=[scale_spec, scale_spec, factor_spec, kept_spec, kept_spec],
         out_specs=factor_spec,
-        compiler_params=pltpu.CompilerParams(vmem_limit_bytes=32 * MIB),
+        compiler_params=pltpu.CompilerParams(vmem_limit_bytes=60 * MIB),
     )(
         post.reshape(rows_all, LANES),
         mean.reshape(rows_all, LANES),

time: 272 us -> 253 us (0.930)
  Pallas kernels: 260 us -> 248 us
  local copies, waits for them, and re-layouts: 9.47 us -> 3.42 us
    pallas_call x1, Pallas kernels: 240 us -> 230 us  [on_device_fused(): pl.pallas_call(functools.partial(messages_kernel, devices, window), out_s...]
    unnamed x13 -> x5, local copies, waits for them, and re-layouts: 7.18 us -> 1.13 us
    pallas_call x1, Pallas kernels: 20.6 us -> 17.8 us  [on_device_fused(): pl.pallas_call(functools.partial(counts_kernel, factor), grid=(blocks //...]
where the time goes in v2:
time: 253 us
  Pallas kernels  248 us (98%)
  local copies, waits for them, and re-layouts  3.42 us (1%)
    pallas_call x1, Pallas kernels, on_device_fused(): pl.pallas_call(functools.partial(messages_kernel, devices, window), out_s...  230 us
    pallas_call x1, Pallas kernels, on_device_fused(): pl.pallas_call(functools.partial(counts_kernel, factor), grid=(blocks //...  17.8 us

profile of v2, /device:TPU:0, one launch (start us, length us, event | category | flops | bytes accessed | tf_op | source)
XLA Modules:
  0.0 253.1 jit_solution(3410945074562387722)
XLA Ops:
  0.6 0.0 copy-start
  0.6 0.8 eq.10
  1.5 0.2 copy-done
  1.6 0.9 fusion
  2.5 230.3 %shard_map.85 = (bf16[32,4,32,512]{3,2,1,0:T(8,128)(2,1)}, bf16[32,4,32,512]{3,2,1,0:T(8,128)(2,1)}, bf16[32,16384]{1,0:T(8,128)(2,1)}, f32[4,32,128]{2,1,0:T(8,...) custom-call(bf16[32,16384]{1,0:T(8,128)(2,1)} %alpha_hbm.1, bf16[32,16384]{1,0:T(8,128)(2,1)} %beta_hbm.1, ...), custom_call_target="tpu_custom_call" | custom-call | tf_op jit(solution)/shard_map/pallas_call | solution.py:421
  232.8 1.5 log_reduce_fusion
  234.3 0.0 copy-start.1
  234.3 17.8 %shard_map.86 = bf16[32,512,512]{2,1,0:T(8,128)(2,1)} custom-call(f32[128,128]{1,0:T(8,128)} %bitcast.9, f32[128,128]{1,0:T(8,128)} %bitcast.10, bf16[32,512,512]{2,1,0:T(8,128)(2,1)} %left_ref.1, bf16[32,128,512]{2,1,0:T(8,128)(2,1)} %bitcast.6, bf16[32,128,512]{2,1,0:T(8,128)(2,1)} %bitcast.7), custom_call_target="tpu_custom_call" | custom-call | tf_op jit(solution)/shard_map/pallas_call | solution.py:469
  252.1 0.0 copy-done.1
  252.1 1.0 copy.10
Async XLA Ops:
  0.6 1.0 copy-start
  234.3 17.8 %copy-start.1 = (bf16[32,16384]{1,0:T(8,128)(2,1)S(1)}, bf16[32,16384]{1,0:T(8,128)(2,1)}, u32[]{:S(2)}) copy-start(bf16[32,16384]{1,0:T(8,128)(2,1)} %get-tuple-element.19) | copy-start | bytes 3145732

commit v3 on v2

--- a/solution.py
+++ b/solution.py
@@ -129,7 +129,7 @@
                 turned = jnp.transpose(jnp.concatenate(picked, axis=0))
                 outbox[chain, k * LANES : (k + 1) * LANES, lanes] = turned.astype(jnp.bfloat16)
 
-        loop(seqs // group, pack)
+        loop(seqs // group, pack, unroll=2)
         loop(devices, lambda i: block_copy(chain, par, lax.rem(i * 7, devices), lambda other: me).start(), 1)
         own_copy(chain, par).start()
 
@@ -160,7 +160,7 @@
                         [shifted[(i - c) % group] for i in range(group)]
                     )
 
-        loop(seqs // group, unpack)
+        loop(seqs // group, unpack, unroll=2)
 
     def small_copy(kind, slot, off, landing):
         other = lax.rem(me + off, devices)
@@ -234,6 +234,7 @@
                 c * per_chunk + i,
                 dot(alpha_first[:, flat(c * per_chunk + i)], right[c * per_chunk + i], 0),
             ),
+            unroll=2,
         )
 
     loop(chunks, first_path)
@@ -254,7 +255,7 @@
             values[steps, b] = emitted.astype(jnp.bfloat16)
             stage(b, dot(values[steps, b], left[b], 1))
 
-        loop(per_chunk, one)
+        loop(per_chunk, one, unroll=2)
 
     loop(chunks, first_back)
     pack_and_send(1, 0)

time: 253 us -> 249 us (0.984)
  Pallas kernels: 248 us -> 244 us
    pallas_call x1, Pallas kernels: 230 us -> 226 us  [on_device_fused(): pl.pallas_call(functools.partial(messages_kernel, devices, window), out_s...]
where the time goes in v3:
time: 249 us
  Pallas kernels  244 us (98%)
  local copies, waits for them, and re-layouts  3.42 us (1%)
    pallas_call x1, Pallas kernels, on_device_fused(): pl.pallas_call(functools.partial(messages_kernel, devices, window), out_s...  226 us
    pallas_call x1, Pallas kernels, on_device_fused(): pl.pallas_call(functools.partial(counts_kernel, factor), grid=(blocks //...  17.8 us

profile of v3, /device:TPU:0, one launch (start us, length us, event | category | flops | bytes accessed | tf_op | source)
XLA Modules:
  0.0 249.0 jit_solution(129500811786582246)
XLA Ops:
  0.6 0.0 copy-start
  0.6 0.8 eq.10
  1.5 0.2 copy-done
  1.6 0.9 fusion
  2.5 226.3 %shard_map.85 = (bf16[32,4,32,512]{3,2,1,0:T(8,128)(2,1)}, bf16[32,4,32,512]{3,2,1,0:T(8,128)(2,1)}, bf16[32,16384]{1,0:T(8,128)(2,1)}, f32[4,32,128]{2,1,0:T(8,...) custom-call(bf16[32,16384]{1,0:T(8,128)(2,1)} %alpha_hbm.1, bf16[32,16384]{1,0:T(8,128)(2,1)} %beta_hbm.1, ...), custom_call_target="tpu_custom_call" | custom-call | tf_op jit(solution)/shard_map/pallas_call | solution.py:422
  228.8 1.5 log_reduce_fusion
  230.3 0.0 copy-start.1
  230.3 17.8 %shard_map.86 = bf16[32,512,512]{2,1,0:T(8,128)(2,1)} custom-call(f32[128,128]{1,0:T(8,128)} %bitcast.9, f32[128,128]{1,0:T(8,128)} %bitcast.10, bf16[32,512,512]{2,1,0:T(8,128)(2,1)} %left_ref.1, bf16[32,128,512]{2,1,0:T(8,128)(2,1)} %bitcast.6, bf16[32,128,512]{2,1,0:T(8,128)(2,1)} %bitcast.7), custom_call_target="tpu_custom_call" | custom-call | tf_op jit(solution)/shard_map/pallas_call | solution.py:470
  248.0 0.0 copy-done.1
  248.0 1.0 copy.10
Async XLA Ops:
  0.6 1.0 copy-start
  230.3 17.8 %copy-start.1 = (bf16[32,16384]{1,0:T(8,128)(2,1)S(1)}, bf16[32,16384]{1,0:T(8,128)(2,1)}, u32[]{:S(2)}) copy-start(bf16[32,16384]{1,0:T(8,128)(2,1)} %get-tuple-element.19) | copy-start | bytes 3145732
